TPU v7x, 32 devices: a whole 2x2x4 slice. The times are simulated.
32 devices in a mesh: expert: 8 (over y, x, core), dp: 4 (over z).
Axes of the slice: x: 2, y: 2, z: 4, core: 2. Of those that a mesh axis runs over, the one named last changes fastest.
Arguments:
- tokens: bfloat16 [512, 2048], P(('dp', 'expert')), may hold values from -6 to 6
- cotangent: bfloat16 [512, 8, 384], P(('dp', 'expert')), may hold values from -1 to 1
- expert_ids: int32 [512, 8], P(('dp', 'expert')), may hold values from 0 to 31, all different within a row; in each aligned block of 16 rows (0 to 15, 16 to 31, ...) at most 5 rows name the same one
- placement: int32 [64], replicated, may hold values from 0 to 31, as said below
- master: float32 [32, 1572864], P(None, ('dp', 'expert')), may hold values from -0.125 to 0.125
- first_moment: float32 [32, 1572864], P(None, ('dp', 'expert')), may hold values from -12 to 12
- second_moment: float32 [32, 1572864], P(None, ('dp', 'expert')), may hold values from 1 to 30
Outputs:
- new_master: float32 [32, 1572864], P(None, ('dp', 'expert'))
- new_first: float32 [32, 1572864], P(None, ('dp', 'expert'))
- new_second: float32 [32, 1572864], P(None, ('dp', 'expert'))
- replica_grad: float32 [64, 384, 4096], P('expert', 'dp')
Inputs may be any that keep to these rules, and one draw needn't show every extreme that they name: `expert_ids`: among the tokens of one device no expert is named more than 5 times; some device names some expert exactly 5 times. `placement`: every one of the 32 experts holds at least one of the 64 slots.
All inputs are finite; a program needn't handle non-finite values.
Results may differ from a plain program's by a relative error of at most 0.017.
Values may be sent and summed in bfloat16 or wider, within the bound.
A program may use at most 192 MiB of HBM per device.

v0:
```python
import jax
import jax.numpy as jnp
from jax import lax
from jax.sharding import PartitionSpec as P

MOST = 5


beta_first = 0.9
beta_second = 0.95
learning_rate = 0.01
decay_rate = 0.1
epsilon = 1e-08
adam_steps = 20.0


def adamw_update(master, first_moment, second_moment, grads):
    new_first = beta_first * first_moment + (1.0 - beta_first) * grads
    new_second = beta_second * second_moment + (1.0 - beta_second) * grads * grads
    corr_first = 1.0 - beta_first**adam_steps
    corr_second = 1.0 - beta_second**adam_steps
    update = (
        new_first / corr_first / (jnp.sqrt(new_second / corr_second) + epsilon)
        + decay_rate * master
    )
    return (master - learning_rate * update, new_first, new_second)


def local(tokens, cotangent, expert_ids, placement, master, first_moment, second_moment):
    expert_devices = lax.axis_size("expert")
    source_index = lax.axis_index("expert")
    slot_count = placement.shape[0]
    slot_local = slot_count // expert_devices
    expert_count = master.shape[0]
    shard_width = master.shape[1]
    token_rows = tokens.shape[0]
    model_width = tokens.shape[1]
    top_count = expert_ids.shape[1]
    hidden_width = cotangent.shape[2]
    assigned = token_rows * top_count
    piece_rows = shard_width * expert_devices // (2 * model_width)
    send_total = slot_count * MOST
    expert_range = jnp.arange(expert_count, dtype=jnp.int32)
    slot_range = jnp.arange(slot_count, dtype=jnp.int32)
    slot_hot = placement[:, None] == expert_range[None, :]
    replicas = jnp.sum(slot_hot.astype(jnp.int32), axis=0)
    earlier_same = (slot_range[:, None] > slot_range[None, :]) & (
        placement[:, None] == placement[None, :]
    )
    slot_rank = jnp.sum(earlier_same.astype(jnp.int32), axis=1)
    wanted = jnp.mod(source_index, replicas)
    target_hot = slot_hot & (slot_rank[:, None] == wanted[None, :])
    target_slot = jnp.sum(jnp.where(target_hot, slot_range[:, None], 0), axis=0)
    flat_ids = expert_ids.reshape(assigned)
    expert_hot = flat_ids[:, None] == expert_range[None, :]
    earlier = jnp.cumsum(expert_hot.astype(jnp.int32), axis=0) - 1
    position = jnp.sum(jnp.where(expert_hot, earlier, 0), axis=1)
    destination = jnp.sum(jnp.where(expert_hot, target_slot[None, :], 0), axis=1)
    target_device = destination // slot_local
    local_slot = destination % slot_local
    send_row = (local_slot * expert_devices + target_device) * MOST + position
    copy_range = jnp.arange(assigned, dtype=jnp.int32)
    row_match = jnp.arange(send_total, dtype=jnp.int32)[:, None] == send_row[None, :]
    filled = jnp.any(row_match, axis=1)
    source_copy = jnp.sum(jnp.where(row_match, copy_range[None, :], 0), axis=1)
    gathered_x = jnp.take(tokens, source_copy // top_count, axis=0)
    send_x = jnp.where(filled[:, None], gathered_x, jnp.zeros_like(gathered_x))
    send_x = send_x.reshape(slot_local, expert_devices, MOST, model_width)
    gathered_dh = jnp.take(cotangent.reshape(assigned, hidden_width), source_copy, axis=0)
    send_dh = jnp.where(filled[:, None], gathered_dh, jnp.zeros_like(gathered_dh))
    send_dh = send_dh.reshape(slot_local, expert_devices, MOST, hidden_width)
    piece_expert = placement.reshape(expert_devices, slot_local).T
    send_weight = master[piece_expert].astype(jnp.bfloat16)
    recv_weight = lax.all_to_all(send_weight, "expert", split_axis=1, concat_axis=1, tiled=True)
    recv_x, recv_dh = (
        lax.all_to_all(send_x, "expert", split_axis=1, concat_axis=1, tiled=True),
        lax.all_to_all(send_dh, "expert", split_axis=1, concat_axis=1, tiled=True),
    )
    rows_x = recv_x.reshape(slot_local, expert_devices * MOST, model_width)
    rows_dh = recv_dh.reshape(slot_local, expert_devices * MOST, hidden_width)
    own_piece = recv_weight.reshape(slot_local, piece_rows, 2 * model_width)
    replica = lax.all_gather(own_piece, "dp", axis=1, tiled=True)
    replica_split = replica.reshape(slot_local, hidden_width, 2, model_width)
    both_values = jnp.einsum(
        "lrd,lcgd->lrgc", rows_x, replica_split, preferred_element_type=jnp.float32
    )
    gate_value = both_values[:, :, 0, :]
    up_value = both_values[:, :, 1, :]
    sigmoid_value = jax.nn.sigmoid(gate_value)
    activation = gate_value * sigmoid_value
    derivative = sigmoid_value * (1.0 + gate_value * (1.0 - sigmoid_value))
    d_gate = (rows_dh * up_value * derivative).astype(jnp.bfloat16)
    d_up = (rows_dh * activation).astype(jnp.bfloat16)
    d_both = jnp.stack([d_gate, d_up], axis=2)
    grad_block = jnp.einsum("lrgc,lrd->clgd", d_both, rows_x, preferred_element_type=jnp.float32)
    summed_rows = lax.psum_scatter(
        grad_block.reshape(lax.axis_size("dp") * piece_rows, slot_local, 2 * model_width).astype(
            jnp.bfloat16
        ),
        "dp",
        scatter_dimension=0,
        tiled=True,
    ).astype(jnp.float32)
    replica_grad = jnp.swapaxes(summed_rows, 0, 1)
    outgoing = replica_grad.reshape(slot_local, expert_devices, shard_width)
    incoming = lax.all_to_all(
        outgoing.astype(jnp.bfloat16), "expert", split_axis=1, concat_axis=1, tiled=True
    ).astype(outgoing.dtype)
    by_slot = jnp.swapaxes(incoming, 0, 1).reshape(slot_count, shard_width)
    grads = jnp.dot(
        slot_hot.T.astype(jnp.float32),
        by_slot,
        precision=lax.Precision.HIGHEST,
        preferred_element_type=jnp.float32,
    )
    new_master, new_first, new_second = adamw_update(master, first_moment, second_moment, grads)
    return (new_master, new_first, new_second, replica_grad)


def solution(mesh):
    return jax.shard_map(
        local,
        mesh=mesh,
        in_specs=(
            P(("dp", "expert"), None),
            P(("dp", "expert"), None, None),
            P(("dp", "expert"), None),
            P(),
            P(None, ("dp", "expert")),
            P(None, ("dp", "expert")),
            P(None, ("dp", "expert")),
        ),
        out_specs=(
            P(None, ("dp", "expert")),
            P(None, ("dp", "expert")),
            P(None, ("dp", "expert")),
            P("expert", "dp", None),
        ),
        check_vma=False,
    )
```

profile of v0, /device:TPU:0, one launch (start us, length us, event | category | flops | bytes accessed | tf_op | source)
XLA Modules:
  0.0 1169.0 jit_solution(9352320237403845544)
XLA Ops:
  8.1 15.3 %gather_fusion.2 = bf16[64,49152]{1,0:T(8,128)(2,1)} fusion(f32[32,49152]{1,0:T(8,128)} %param.11, s32[1024]{0:T(1024)S(1)} %pad_clamp_fusion), kind=kCustom, calls=%fused_computation.2 | custom fusion | bytes 12583168 | tf_op jit(solution)/shard_map/gather | solution.py:73
  23.5 6.4 copy.54
  29.9 76.5 %all_to_all.20 = bf16[8,8,49152]{2,0,1:T(8,128)(2,1)S(1)} all-to-all(bf16[8,8,49152]{2,0,1:T(8,128)(2,1)S(1)} %copy.54), channel_id=1, replica_groups=mesh['expert'=8,'dp'=4] {'expert'}, dimensions={1} | all-to-all | bytes 12582912 | tf_op jit(solution)/shard_map/all_to_all | solution.py:74
  106.4 6.1 copy.55
  112.5 12.4 %reshape.200 = bf16[8,96,4096]{2,1,0:T(8,128)(2,1)} reshape(bf16[8,8,49152]{2,1,0:T(8,128)(2,1)} %copy.55) | data formatting | bytes 12582912 | tf_op jit(solution)/shard_map/reshape | solution.py:81
  127.5 2.0 gather_fusion.1
  130.8 4.0 all-to-all-start.1
  134.9 2.4 gather_fusion
  138.4 1.9 copy.51
  140.3 1.4 all-to-all-done.1
  141.6 3.6 all-to-all-start
  145.5 1.0 bitcast_convert_fusion
  146.5 402.8 %all-gather.2.cloned.1.call-done = bf16[8,384,4096]{2,1,0:T(8,128)(2,1)} async-done(((bf16[8,96,4096]{2,1,0:T(8,128)(2,1)}), bf16[8,384,4096]{2,1,0:T(8,128)(2,1)}) %all-gather.2.cloned.1.call-update) | async-done | bytes 25165840 | tf_op jit(solution)/shard_map/all_gather | solution.py:82
  549.3 32.6 %copy.56 = bf16[8,384,4096]{1,2,0:T(8,128)(2,1)} copy(bf16[8,384,4096]{2,1,0:T(8,128)(2,1)} %all-gather.2.cloned.1.call-done) | data formatting | bytes 50331648 | tf_op jit(solution)/shard_map/all_gather | solution.py:82
  582.0 10.4 convolution_bitcast_fusion
  592.7 11.8 %convolution_convert_fusion = bf16[8,2048,2,384]{3,1,2,0:T(8,128)(2,1)} fusion(bf16[8,40,2048,1]{2,0,1,3:T(8,128)(2,1)S(1)} %bitcast.35, bf16[8,40,1,384]{3,1,2,0:T(8,128)(2,1)S(1)} %get-tuple-element.12, bf16[8,40,1,384]{3,1,2,0:T(8,128)(2,1)S(1)} %get-tuple-element.11), kind=kOutput, calls=%fused_computation.3 | convolution fusion | flops 1020198912 | bytes 26968064 | tf_op jit(solution)/shard_map/lrgc,lrd->clgd/dot_general | solution.py:95
  604.4 30.7 %copy.62 = bf16[384,8,4096]{2,0,1:T(8,128)(2,1)} copy(bf16[384,8,4096]{0,2,1:T(8,128)(2,1)} %bitcast.30) | data formatting | bytes 50331648 | tf_op jit(solution)/shard_map/convert_element_type | solution.py:97
  635.2 412.7 %reduce-scatter.2.cloned.1.call-done = bf16[96,8,4096]{2,0,1:T(8,128)(2,1)} async-done(((bf16[384,8,4096]{2,0,1:T(8,128)(2,1)}), bf16[96,8,4096]{2,0,1:T(8,128)(2,1)}) %reduce-scatter.2.cloned.1.call-update) | async-done | bytes 6291472 | tf_op jit(solution)/shard_map/reduce_scatter | solution.py:96
  1047.9 12.4 %convert_element_type.62 = bf16[8,8,49152]{2,1,0:T(8,128)(2,1)} reshape(bf16[8,96,4096]{2,1,0:T(8,128)(2,1)} %bitcast.33) | data formatting | bytes 12582912 | tf_op jit(solution)/shard_map/convert_element_type | solution.py:107
  1060.3 8.9 copy.63
  1069.2 5.0 all-to-all-start.3
  1074.2 9.3 bitcast_convert_fusion.1
  1083.5 62.3 %all-to-all-done.3 = bf16[8,8,49152]{2,0,1:T(8,128)(2,1)} async-done(((bf16[8,8,49152]{2,0,1:T(8,128)(2,1)}), bf16[8,8,49152]{2,0,1:T(8,128)(2,1)}, u32[]{:S(2)}, u32[]{:S(2)}) %all-to-all-start.3) | async-done | bytes 6291488 | tf_op jit(solution)/shard_map/all_to_all | solution.py:106
  1145.8 15.9 %multiply_subtract_fusion = (f32[32,49152]{1,0:T(8,128)}, f32[32,49152]{1,0:T(8,128)}, f32[32,49152]{1,0:T(8,128)}) fusion(f32[32,49152]{1,0:T(8,128)} %param.11, f32[32,49152]{1,0:T(8,128)} %param.12, f32[32,49152]{1,0:T(8,128)} %param.13, bf16[8,8,49152]{2,0,1:T(8,128)(2,1)} %all-to-all-done.3, s32[64]{0:T(128)S(1)} %copy-done.4), kind=kOutput, calls=%fused_computation.9 | convolution fusion | flops 224921600 | bytes 44040448 | tf_op jit(solution)/shard_map/dot_general | solution.py:110
  (43 shorter events, 6.3 us)
Async XLA Ops:
  7.2 120.4 %copy-start = (bf16[16,8,384]{2,1,0:T(8,128)(2,1)S(1)}, bf16[16,8,384]{2,1,0:T(8,128)(2,1)}, u32[]{:S(2)}) copy-start(bf16[16,8,384]{2,1,0:T(8,128)(2,1)} %param.8) | copy-start | bytes 294916
  7.2 542.2 %all-gather.2.cloned.1.call-start = ((), (), s32[]{:S(2)}) async-start(), calls=%async_computation.5 | async-start | bytes 31457280 | tf_op jit(solution)/shard_map/all_gather | solution.py:82
  124.9 0.7 copy-start.3
  124.9 1.1 copy-start.4
  124.9 9.9 copy-start.2
  130.8 10.8 all-to-all-start.1
  141.6 440.3 %all-to-all-start = ((bf16[8,8,5,2048]{3,0,2,1:T(8,128)(2,1)}), bf16[8,8,5,2048]{3,0,2,1:T(8,128)(2,1)S(1)}, u32[]{:S(2)}, u32[]{:S(2)}) async-start(bf16[8,8,5,2048]{3,0,2,1:T(8,128)(2,1)} %copy.51), calls=%async_computation | async-start | bytes 2621440 | tf_op jit(solution)/shard_map/all_to_all | solution.py:76
  145.2 902.6 %reduce-scatter.2.cloned.1.call-start = ((), (), s32[]{:S(2)}) async-start(), calls=%async_computation.6 | async-start | bytes 31457280 | tf_op jit(solution)/shard_map/reduce_scatter | solution.py:96
  1069.2 76.6 %all-to-all-start.3 = ((bf16[8,8,49152]{2,0,1:T(8,128)(2,1)}), bf16[8,8,49152]{2,0,1:T(8,128)(2,1)}, u32[]{:S(2)}, u32[]{:S(2)}) async-start(bf16[8,8,49152]{2,0,1:T(8,128)(2,1)} %copy.63), calls=%async_computation.4 | async-start | bytes 12582912 | tf_op jit(solution)/shard_map/all_to_all | solution.py:106
  1145.8 15.9 %copy-start.1 = (bf16[16,8,384]{2,1,0:T(8,128)(2,1)S(1)}, bf16[16,8,384]{2,1,0:T(8,128)(2,1)}, u32[]{:S(2)}) copy-start(bf16[16,8,384]{2,1,0:T(8,128)(2,1)} %param.8) | copy-start | bytes 294916
Sparse Core Ops, SparseCore 0:
  125.1 424.2 all-gather.1
  635.3 412.5 reduce-scatter.1
where the time goes:
time: 1180 us; the launch traced here: 1170 us
  waiting for transfers between devices  879 us (74%)
  local copies, waits for them, and re-layouts  135 us (11%)
  blocking collectives  76.5 us (6%)
  matrix products  38.1 us (3%)
  between operations  14.7 us (1%)
  starting transfers between devices  12.9 us (1%)
  other arithmetic  12.7 us (1%)
    reduce_scatter x1, waiting for transfers between devices, local(): lax.psum_scatter(grad_block.reshape(lax.axis_size('dp') * piece_rows, slo...  413 us
    all_gather x1, waiting for transfers between devices, local(): replica = lax.all_gather(own_piece, 'dp', axis=1, tiled=True)  403 us
    all_to_all x1, blocking collectives, local(): lax.all_to_all(send_weight, 'expert', split_axis=1, concat_axis=1, tiled=...  76.5 us
    all_to_all x1, waiting for transfers between devices, local(): lax.all_to_all(outgoing.astype(jnp.bfloat16), 'expert', split_axis=1, con...  62.3 us
    all_gather x1, local copies, waits for them, and re-layouts, local(): replica = lax.all_gather(own_piece, 'dp', axis=1, tiled=True)  32.6 us
    convert_element_type x1, local copies, waits for them, and re-layouts, local(): grad_block.reshape(lax.axis_size('dp') * piece_rows, slot_local, 2 * mode...  30.7 us
  transfers between devices with their start and end apart: 5, of which 4 were waited for; matrix products, arithmetic and copies ran while one was open for 5% of the time, Pallas kernels for 0%

commit v1 on v0

--- a/solution.py
+++ b/solution.py
@@ -1,6 +1,10 @@
+import functools
+
 import jax
 import jax.numpy as jnp
 from jax import lax
+from jax.experimental import pallas as pl
+from jax.experimental.pallas import tpu as pltpu
 from jax.sharding import PartitionSpec as P
 
 MOST = 5
@@ -26,7 +30,7 @@
     return (master - learning_rate * update, new_first, new_second)
 
 
-def local(tokens, cotangent, expert_ids, placement, master, first_moment, second_moment):
+def move_weights(tokens, cotangent, expert_ids, placement, master, first_moment, second_moment):
     expert_devices = lax.axis_size("expert")
     source_index = lax.axis_index("expert")
     slot_count = placement.shape[0]
@@ -117,6 +121,228 @@
     return (new_master, new_first, new_second, replica_grad)
 
 
+NT = (((1,), (1,)), ((), ()))
+VMEM_LIMIT = 56 * 1024 * 1024
+
+
+def block_count(units, most):
+    blocks = 1
+    while units % blocks or units // blocks > most:
+        blocks += 1
+    return blocks
+
+
+def hidden_kernel(units, top, master, tokens, packed, dense, compact, turned):
+    step = pl.program_id(0)
+    experts = master.shape[0]
+    width = tokens.shape[1]
+    total = tokens.shape[0]
+    here = master.shape[1] // (2 * width)
+
+    @pl.when(step == 0)
+    def _():
+        turned[...] = packed[...].astype(jnp.float32).T
+
+    names = turned[units * top : (units + 1) * top, :]
+    expert_row = lax.broadcasted_iota(jnp.int32, (experts, total), 0).astype(jnp.float32)
+    hot = [(names[a : a + 1, :] == expert_row).astype(jnp.float32) for a in range(top)]
+    weights = jnp.concatenate(
+        [master[:, c * width : (c + 1) * width].astype(jnp.bfloat16) for c in range(2 * here)],
+        axis=0,
+    )
+    values = lax.dot_general(weights, tokens[...], NT, preferred_element_type=jnp.float32)
+    for u in range(here):
+        gate = values[2 * u * experts : (2 * u + 1) * experts]
+        up = values[(2 * u + 1) * experts : (2 * u + 2) * experts]
+        start = pl.multiple_of((step * here + u) * top, top)
+        cot_rows = turned[pl.ds(start, top), :]
+        cot = cot_rows[0:1, :] * hot[0]
+        for a in range(1, top):
+            cot = cot + cot_rows[a : a + 1, :] * hot[a]
+        sig = 1.0 / (1.0 + jnp.exp(-gate))
+        d_gate = cot * up * (sig * (1.0 + gate * (1.0 - sig)))
+        d_up = cot * (gate * sig)
+        dense[2 * u * experts : (2 * u + 1) * experts, :] = d_gate.astype(jnp.bfloat16)
+        dense[(2 * u + 1) * experts : (2 * u + 2) * experts, :] = d_up.astype(jnp.bfloat16)
+        picked = [
+            jnp.sum(d * hot[a], axis=0, keepdims=True) for d in (d_gate, d_up) for a in range(top)
+        ]
+        compact[2 * u * top : (2 * u + 2) * top, :] = jnp.concatenate(picked, axis=0).astype(
+            jnp.bfloat16
+        )
+
+
+def update_kernel(dense, tokens, master, first, second, new_master, new_first, new_second):
+    experts = master.shape[0]
+    width = tokens.shape[1]
+    grads = jnp.dot(dense[...], tokens[...], preferred_element_type=jnp.float32)
+    for c in range(master.shape[1] // width):
+        cols = slice(c * width, (c + 1) * width)
+        results = adamw_update(
+            master[:, cols],
+            first[:, cols],
+            second[:, cols],
+            grads[c * experts : (c + 1) * experts],
+        )
+        new_master[:, cols], new_first[:, cols], new_second[:, cols] = results
+
+
+def replica_kernel(top, mask, spread, tokens, out, fold):
+    width = tokens.shape[1]
+    units = out.shape[1]
+    rows = spread.shape[0]
+
+    @pl.when(pl.program_id(0) == 0)
+    def _():
+        out_row = lax.broadcasted_iota(jnp.int32, fold.shape, 0)
+        in_row = lax.broadcasted_iota(jnp.int32, fold.shape, 1) // top
+        wanted = (in_row % 2) * units + in_row // 2
+        fold[...] = (out_row == wanted).astype(jnp.bfloat16)
+
+    both = jnp.concatenate([mask[0], mask[0]], axis=0)
+    masked = spread[...].reshape(rows // (2 * top), 2 * top, -1) * both[None]
+    chosen = jnp.dot(
+        fold[...], masked.reshape(rows, -1), preferred_element_type=jnp.float32
+    ).astype(jnp.bfloat16)
+    grad = jnp.dot(chosen, tokens[...], preferred_element_type=jnp.float32)
+    out[0, :, :width] = grad[:units]
+    out[0, :, width:] = grad[units:]
+
+
+def params():
+    return pltpu.CompilerParams(
+        dimension_semantics=("arbitrary",), vmem_limit_bytes=VMEM_LIMIT
+    )
+
+
+def hidden_grads(units, top, master, tokens, packed):
+    experts, shard = master.shape
+    total = tokens.shape[0]
+    blocks = block_count(units, 3)
+    here = units // blocks
+    return pl.pallas_call(
+        functools.partial(hidden_kernel, units, top),
+        grid=(blocks,),
+        in_specs=[
+            pl.BlockSpec((experts, shard // blocks), lambda i: (0, i)),
+            pl.BlockSpec(tokens.shape, lambda i: (0, 0)),
+            pl.BlockSpec(packed.shape, lambda i: (0, 0)),
+        ],
+        out_specs=[
+            pl.BlockSpec((2 * here * experts, total), lambda i: (i, 0)),
+            pl.BlockSpec((2 * here * top, total), lambda i: (i, 0)),
+        ],
+        out_shape=[
+            jax.ShapeDtypeStruct((2 * units * experts, total), jnp.bfloat16),
+            jax.ShapeDtypeStruct((2 * units * top, total), jnp.bfloat16),
+        ],
+        scratch_shapes=[pltpu.VMEM((packed.shape[1], total), jnp.float32)],
+        compiler_params=params(),
+        name="hidden_grads",
+    )(master, tokens, packed)
+
+
+def update_shards(units, dense, tokens, master, first, second):
+    experts, shard = master.shape
+    total = tokens.shape[0]
+    blocks = block_count(units, 2)
+    state = pl.BlockSpec((experts, shard // blocks), lambda i: (0, i))
+    return pl.pallas_call(
+        update_kernel,
+        grid=(blocks,),
+        in_specs=[
+            pl.BlockSpec((dense.shape[0] // blocks, total), lambda i: (i, 0)),
+            pl.BlockSpec(tokens.shape, lambda i: (0, 0)),
+            state,
+            state,
+            state,
+        ],
+        out_specs=[state] * 3,
+        out_shape=[jax.ShapeDtypeStruct(master.shape, jnp.float32)] * 3,
+        compiler_params=params(),
+        cost_estimate=pl.CostEstimate(
+            flops=2 * dense.shape[0] * total * tokens.shape[1],
+            bytes_accessed=24 * master.size,
+            transcendentals=0,
+        ),
+        name="update_shards",
+    )(dense, tokens, master, first, second)
+
+
+def replica_grads(units, top, mask, spread, tokens):
+    slots, _, total = mask.shape
+    width = tokens.shape[1]
+    return pl.pallas_call(
+        functools.partial(replica_kernel, top),
+        grid=(slots,),
+        in_specs=[
+            pl.BlockSpec((1, top, total), lambda i: (i, 0, 0)),
+            pl.BlockSpec(spread.shape, lambda i: (0, 0)),
+            pl.BlockSpec(tokens.shape, lambda i: (0, 0)),
+        ],
+        out_specs=pl.BlockSpec((1, units, 2 * width), lambda i: (i, 0, 0)),
+        out_shape=jax.ShapeDtypeStruct((slots, units, 2 * width), jnp.float32),
+        scratch_shapes=[pltpu.VMEM((2 * units, spread.shape[0]), jnp.bfloat16)],
+        compiler_params=params(),
+        name="replica_grads",
+    )(mask, spread, tokens)
+
+
+def slot_masks(placement, names, expert_count, slot_local, token_rows):
+    expert_devices = lax.axis_size("expert")
+    slot_count = placement.shape[0]
+    slot_range = jnp.arange(slot_count, dtype=jnp.int32)
+    same = placement[:, None] == placement[None, :]
+    replicas = jnp.sum(same.astype(jnp.int32), axis=1)
+    earlier = same & (slot_range[:, None] > slot_range[None, :])
+    rank = jnp.sum(earlier.astype(jnp.int32), axis=1)
+    first_slot = lax.axis_index("expert") * slot_local
+    own = lambda values: lax.dynamic_slice_in_dim(values, first_slot, slot_local)
+    source = jnp.arange(names.shape[1], dtype=jnp.int32) // token_rows % expert_devices
+    chosen = source[None, :] % own(replicas)[:, None] == own(rank)[:, None]
+    held = own(placement)[:, None, None].astype(names.dtype) == names[None]
+    return (held & chosen[:, None, :]).astype(jnp.bfloat16)
+
+
+def move_tokens(tokens, cotangent, expert_ids, placement, master, first_moment, second_moment):
+    axes = ("dp", "expert")
+    devices = lax.axis_size("dp") * lax.axis_size("expert")
+    token_rows, width = tokens.shape
+    top, hidden = cotangent.shape[1:]
+    experts, shard = master.shape
+    units = shard // (2 * width)
+    slot_local = placement.shape[0] // lax.axis_size("expert")
+    pieces = cotangent.reshape(token_rows, top, devices, units).transpose(2, 0, 3, 1)
+    pieces = pieces.reshape(devices, token_rows, units * top)
+    names = jnp.broadcast_to(expert_ids.astype(jnp.bfloat16)[None], (devices, token_rows, top))
+    lanes = (units + 1) * top
+    packed = jnp.concatenate([pieces, names], axis=2)
+    packed = jnp.pad(packed, ((0, 0), (0, 0), (0, -lanes % 128)))
+    packed = lax.all_to_all(packed, axes, split_axis=0, concat_axis=0, tiled=True)
+    packed = packed.reshape(devices * token_rows, -1)
+    all_tokens = lax.all_gather(tokens, axes, axis=0, tiled=True)
+    dense, compact = hidden_grads(units, top, master, all_tokens, packed)
+    spread = lax.all_gather(compact, "expert", axis=0, tiled=True)
+    states = update_shards(units, dense, all_tokens, master, first_moment, second_moment)
+    all_names = packed[:, units * top : lanes].T
+    mask = slot_masks(placement, all_names, experts, slot_local, token_rows)
+    replica_grad = replica_grads(
+        units * lax.axis_size("expert"), top, mask, spread, all_tokens
+    )
+    return (*states, replica_grad)
+
+
+def local(tokens, cotangent, expert_ids, placement, master, first_moment, second_moment):
+    devices = lax.axis_size("dp") * lax.axis_size("expert")
+    token_values = tokens.size * devices
+    weight_values = placement.shape[0] // lax.axis_size("expert") * cotangent.shape[2] * 2 * tokens.shape[1]
+    whole_units = master.shape[1] % (2 * tokens.shape[1]) == 0
+    few = token_values < weight_values and tokens.shape[0] * devices % 128 == 0
+    exact = master.shape[0] <= 256 and tokens.shape[0] % 16 == 0
+    plan = move_tokens if whole_units and few and exact else move_weights
+    return plan(tokens, cotangent, expert_ids, placement, master, first_moment, second_moment)
+
+
 def solution(mesh):
     return jax.shard_map(
         local,

time: 1180 us -> 122 us (0.10)
  waiting for transfers between devices: 879 us -> 47.7 us
  local copies, waits for them, and re-layouts: 135 us -> 4.81 us
  blocking collectives: 76.5 us -> 15.5 us
  matrix products: 38.1 us -> 0 us
  Pallas kernels: 0 us -> 37.5 us
  starting transfers between devices: 12.9 us -> 0.08 us
    reduce_scatter x1 -> x0, waiting for transfers between devices: 413 us -> none  [local(): lax.psum_scatter(grad_block.reshape(lax.axis_size('dp') * piece_rows, slo...]
    all_gather x1 -> x2, waiting for transfers between devices: 403 us -> 47 us  [the longest x1 41.2 us: move_tokens(): all_tokens = lax.all_gather(tokens, axes, axis=0, tiled=True)]
    all_to_all x3 -> x0, waiting for transfers between devices: 63.6 us -> none  [the longest x1 62.3 us: local(): lax.all_to_all(outgoing.astype(jnp.bfloat16), 'expert', split_axis=1, con...]
    all_to_all x1, blocking collectives: 76.5 us -> 15.5 us  [move_tokens(): lax.all_to_all(packed, axes, split_axis=0, concat_axis=0, tiled=True)]
    convert_element_type x4 -> x1, local copies, waits for them, and re-layouts: 58.4 us -> 0.09 us  [move_tokens(): expert_ids.astype(jnp.bfloat16)[None]]
    dot_general x3 -> x0, matrix products: 38.1 us -> none  [the longest x1 15.9 us: local(): jnp.dot(slot_hot.T.astype(jnp.float32), by_slot, precision=lax.Precision....]
    pallas_call x0 -> x3, Pallas kernels: none -> 37.5 us  [the longest x1 17.3 us: update_shards(): pl.pallas_call(update_kernel, grid=(blocks,), in_specs=[pl.BlockSpec((den...]
    all_gather x1 -> x0, local copies, waits for them, and re-layouts: 32.6 us -> none  [local(): replica = lax.all_gather(own_piece, 'dp', axis=1, tiled=True)]
  transfers between devices with their start and end apart: 5 -> 2, of which waited for: 4 -> 2; matrix products, arithmetic and copies ran while one was open for 5% -> 6% of each run, Pallas kernels for 0% -> 14%
where the time goes in v1:
time: 122 us
  waiting for transfers between devices  47.7 us (39%)
  Pallas kernels  37.5 us (31%)
  blocking collectives  15.5 us (13%)
  between operations  14.1 us (12%)
  local copies, waits for them, and re-layouts  4.81 us (4%)
  other arithmetic  2.14 us (2%)
    all_gather x1, waiting for transfers between devices, move_tokens(): all_tokens = lax.all_gather(tokens, axes, axis=0, tiled=True)  41.2 us
    pallas_call x1, Pallas kernels, update_shards(): pl.pallas_call(update_kernel, grid=(blocks,), in_specs=[pl.BlockSpec((den...  17.3 us
    all_to_all x1, blocking collectives, move_tokens(): lax.all_to_all(packed, axes, split_axis=0, concat_axis=0, tiled=True)  15.5 us
    pallas_call x1, Pallas kernels, replica_grads(): pl.pallas_call(functools.partial(replica_kernel, top), grid=(slots,), in_...  11.7 us
    pallas_call x1, Pallas kernels, hidden_grads(): pl.pallas_call(functools.partial(hidden_kernel, units, top), grid=(blocks...  8.53 us
    all_gather x1, waiting for transfers between devices, move_tokens(): spread = lax.all_gather(compact, 'expert', axis=0, tiled=True)  5.79 us
    reshape x1, local copies, waits for them, and re-layouts, move_tokens(): cotangent.reshape(token_rows, top, devices, units).transpose(2, 0, 3, 1)  3.37 us
  transfers between devices with their start and end apart: 2, of which 2 were waited for; matrix products, arithmetic and copies ran while one was open for 6% of the time, Pallas kernels for 14%

profile of v1, /device:TPU:0, one launch (start us, length us, event | category | flops | bytes accessed | tf_op | source)
XLA Modules:
  0.0 121.8 jit_solution(16103404078513524739)
XLA Ops:
  7.2 0.0 all-gather.3.cloned.1.call-start
  7.2 0.7 all-gather.3.cloned.1.call-update
  7.9 0.0 all-gather.5.cloned.1.call-start
  7.9 0.7 convert_element_type.18
  8.6 0.1 copy.23
  8.7 3.4 %reshape.111 = bf16[16,8,32,12]{3,2,1,0:T(8,128)(2,1)S(1)} reshape(bf16[16,8,384]{2,1,0:T(8,128)(2,1)} %param.8) | data formatting | bytes 196608 | tf_op jit(solution)/shard_map/reshape | solution.py:315
  12.1 0.9 copy.22
  13.0 0.2 copy.24
  13.2 0.1 fusion.2
  13.3 15.5 %all_to_all.5 = bf16[32,16,128]{2,1,0:T(8,128)(2,1)} all-to-all(bf16[32,16,128]{2,1,0:T(8,128)(2,1)S(1)} %fusion.2), channel_id=1, replica_groups=mesh['expert'=8,'dp'=4] {'dp','expert'}, dimensions={0} | all-to-all | bytes 262144 | tf_op jit(solution)/shard_map/all_to_all | solution.py:321
  28.8 41.2 %all-gather.3.cloned.1.call-done.tokens = bf16[512,2048]{1,0:T(8,128)(2,1)} async-done(((bf16[16,2048]{1,0:T(8,128)(2,1)}), bf16[512,2048]{1,0:T(8,128)(2,1)}) %all-gather.3.cloned.1.call-update) | async-done | bytes 2097168 | tf_op jit(solution)/shard_map/all_gather | solution.py:323
  70.0 8.5 %hidden_grads.1 = (bf16[768,512]{1,0:T(8,128)(2,1)}, bf16[192,512]{1,0:T(8,128)(2,1)}) custom-call(f32[32,49152]{1,0:T(8,128)} %master.3, bf16[512,2048]{1,0:T(8,128)(2,1)} %all-gather.3.cloned.1.call-done.tokens, bf16[512,128]{1,0:T(8,128)(2,1)} %bitcast.7), custom_call_target="tpu_custom_call" | custom-call | tf_op jit(solution)/shard_map/hidden_grads/pallas_call | solution.py:223
  78.5 0.0 all-gather.5.cloned.1.call-update
  78.6 0.2 fusion.3
  78.8 0.1 dynamic_slice.11
  78.8 0.1 dynamic-slice_convert_fusion
  78.9 0.1 broadcast_compare_fusion
  79.0 0.3 fusion.4
  79.3 0.1 slice_bitcast_fusion
  79.4 0.1 copy.25
  79.5 0.7 and_convert_fusion.mask
  80.2 17.3 %update_shards.1 = (f32[32,49152]{1,0:T(8,128)}, f32[32,49152]{1,0:T(8,128)}, f32[32,49152]{1,0:T(8,128)}) custom-call(bf16[768,512]{1,0:T(8,128)(2,1)} %get-tuple-element.9.dense, bf16[512,2048]{1,0:T(8,128)(2,1)} %all-gather.3.cloned.1.call-done.tokens, f32[32,49152]{1,0:T(8,128)} %master.3, f32[32,49152]{1,0:T(8,128)} %first.1, f32[32,49152]{1,0:T(8,128)} %second.1), custom_call_target="tpu_custom_call" | custom-call | flops 1610612736 | bytes 37748736 | tf_op jit(solution)/shard_map/update_shards/pallas_call | solution.py:250
  97.5 5.8 %all-gather.5.cloned.1.call-done.spread = bf16[1536,512]{1,0:T(8,128)(2,1)} async-done(((bf16[192,512]{1,0:T(8,128)(2,1)}), bf16[1536,512]{1,0:T(8,128)(2,1)}) %all-gather.5.cloned.1.call-update) | async-done | bytes 1572880 | tf_op jit(solution)/shard_map/all_gather | solution.py:325
  103.3 11.7 %replica_grads.1 = f32[8,96,4096]{2,1,0:T(8,128)} custom-call(bf16[8,8,512]{2,1,0:T(8,128)(2,1)} %and_convert_fusion.mask, bf16[1536,512]{1,0:T(8,128)(2,1)} %all-gather.5.cloned.1.call-done.spread, bf16[512,2048]{1,0:T(8,128)(2,1)} %all-gather.3.cloned.1.call-done.tokens), custom_call_target="tpu_custom_call" | custom-call | tf_op jit(solution)/shard_map/replica_grads/pallas_call | solution.py:275
  (6 shorter events, 0.0 us)
Async XLA Ops:
  7.2 62.9 %all-gather.3.cloned.1.call-start = ((), (), s32[]{:S(2)}) async-start(), calls=%async_computation.1 | async-start | bytes 2162688 | tf_op jit(solution)/shard_map/all_gather | solution.py:323
  7.9 95.4 %all-gather.5.cloned.1.call-start = ((), (), s32[]{:S(2)}) async-start(), calls=%async_computation.2 | async-start | bytes 1769472 | tf_op jit(solution)/shard_map/all_gather | solution.py:325
  8.7 69.9 %copy-start.1 = (s32[64]{0:T(128)S(1)}, s32[64]{0:T(128)}, u32[]{:S(2)}) copy-start(s32[64]{0:T(128)} %param.10) | copy-start | bytes 772
  28.8 50.5 %copy-start = (bf16[32,16,128]{2,1,0:T(8,128)(2,1)S(1)}, bf16[32,16,128]{2,1,0:T(8,128)(2,1)}, u32[]{:S(2)}) copy-start(bf16[32,16,128]{2,1,0:T(8,128)(2,1)} %all_to_all.5) | copy-start | bytes 393220
Sparse Core Ops, SparseCore 0:
  10.9 59.1 all-gather.2
  78.7 24.5 all-gather.4

commit v2 on v0

--- a/solution.py
+++ b/solution.py
@@ -1,6 +1,10 @@
+import functools
+
 import jax
 import jax.numpy as jnp
 from jax import lax
+from jax.experimental import pallas as pl
+from jax.experimental.pallas import tpu as pltpu
 from jax.sharding import PartitionSpec as P
 
 MOST = 5
@@ -26,7 +30,7 @@
     return (master - learning_rate * update, new_first, new_second)
 
 
-def local(tokens, cotangent, expert_ids, placement, master, first_moment, second_moment):
+def move_weights(tokens, cotangent, expert_ids, placement, master, first_moment, second_moment):
     expert_devices = lax.axis_size("expert")
     source_index = lax.axis_index("expert")
     slot_count = placement.shape[0]
@@ -117,6 +121,390 @@
     return (new_master, new_first, new_second, replica_grad)
 
 
+NT = (((1,), (1,)), ((), ()))
+VMEM_LIMIT = 56 * 1024 * 1024
+
+
+def block_count(units, most):
+    blocks = 1
+    while units % blocks or units // blocks > most:
+        blocks += 1
+    return blocks
+
+
+def exchange_kernel(
+    units, pad, blocks, tokens, cot, ids, master,
+    all_tokens, dense, spread, names,
+    held, weights, packed, landed, turned,
+    held_sem, own_sem, row_sems, plane_sems, pair_sems, piece_sems, swap_sems, share_sems,
+):
+    groups, members = lax.axis_size("dp"), lax.axis_size("expert")
+    pairs = members // 2
+    count = groups * members
+    group, member = lax.axis_index("dp"), lax.axis_index("expert")
+    pair, half = member // 2, member % 2
+    me = group * members + member
+    own_rows, width = tokens.shape
+    experts, top = master.shape[0], ids.shape[1]
+    total = all_tokens.shape[0]
+    here = units // blocks
+    block_cols = master.shape[1] // blocks
+
+    def device(g, e):
+        return {"dp": g, "expert": e}
+
+    def remote(source, target, sems, index, to):
+        return pltpu.make_async_remote_copy(
+            src_ref=source, dst_ref=target,
+            send_sem=sems.at[(0, *index)], recv_sem=sems.at[(1, *index)],
+            device_id=to, device_id_type=pl.DeviceIdType.MESH,
+        )
+
+    def shard(h, q, c):
+        owner = ((group + groups - h) % groups) * members + 2 * ((pair + pairs - q) % pairs) + c
+        return all_tokens.at[pl.ds(pl.multiple_of(owner * own_rows, own_rows), own_rows)]
+
+    def along(h):
+        to = device((group + h) % groups, member)
+        return remote(shard(0, 0, half), shard(0, 0, half), row_sems, (h,), to)
+
+    def across(h, q):
+        to = device(group, 2 * ((pair + q) % pairs) + half)
+        return remote(shard(h, 0, half), shard(h, 0, half), plane_sems, (h, q), to)
+
+    def sideways(h, q):
+        to = device(group, 2 * pair + 1 - half)
+        return remote(shard(h, q, half), shard(h, q, half), pair_sems, (h, q), to)
+
+    def piece(step):
+        other = (me + step) % count
+        source = packed.at[pl.ds(pl.multiple_of(other * pad, pad), pad)]
+        target = landed.at[pl.ds(pl.multiple_of(me * pad, pad), pad)]
+        return remote(source, target, piece_sems, (step,), device(other // members, other % members))
+
+    share = 2 * here * top
+
+    def part(b, q, c):
+        owner = 2 * ((pair + pairs - q) % pairs) + c
+        start = owner * (blocks * share) + b * share
+        return spread.at[pl.ds(pl.multiple_of(start, share), share)]
+
+    def swap(b, q):
+        to = device(group, 2 * ((pair + q) % pairs) + half)
+        return remote(part(b, 0, half), part(b, 0, half), swap_sems, (b, q), to)
+
+    def pass_on(b, q):
+        to = device(group, 2 * pair + 1 - half)
+        return remote(part(b, q, half), part(b, q, half), share_sems, (b, q), to)
+
+    loads = []
+    for b in range(blocks):
+        cols = pl.ds(b * block_cols, block_cols)
+        loads.append(pltpu.make_async_copy(master.at[:, cols], held.at[:, cols], held_sem.at[b]))
+    all_tokens[pl.ds(pl.multiple_of(me * own_rows, own_rows), own_rows), :] = tokens[...]
+
+    barrier = pltpu.get_barrier_semaphore()
+
+    @pl.loop(1, count)
+    def _(step):
+        other = (me + step) % count
+        pl.semaphore_signal(
+            barrier, inc=1, device_id=device(other // members, other % members),
+            device_id_type=pl.DeviceIdType.MESH,
+        )
+
+    for load in loads:
+        load.start()
+    pl.semaphore_wait(barrier, count - 1)
+
+    for h in range(1, groups):
+        along(h).start()
+    for q in range(1, pairs):
+        across(0, q).start()
+    sideways(0, 0).start()
+
+    out_row = lax.broadcasted_iota(jnp.int32, (count * pad, cot.shape[1]), 0)
+    in_col = lax.broadcasted_iota(jnp.int32, (count * pad, cot.shape[1]), 1)
+    wanted = (out_row // pad) * units + out_row % pad
+    pick = ((in_col == wanted) & (out_row % pad < units)).astype(jnp.bfloat16)
+    turned_cot = lax.dot_general(pick, cot[...], NT, preferred_element_type=jnp.float32)
+    lane = lax.broadcasted_iota(jnp.int32, (own_rows, own_rows * top), 1)
+    row = lax.broadcasted_iota(jnp.int32, (own_rows, own_rows * top), 0)
+    flat = jnp.zeros((own_rows, own_rows * top), jnp.float32)
+    numbers = ids[...].astype(jnp.float32)
+    for a in range(top):
+        flat = flat + jnp.where(lane == row * top + a, numbers[:, a : a + 1], 0.0)
+    flat = jnp.sum(flat, axis=0, keepdims=True)
+    kind = lax.broadcasted_iota(jnp.int32, turned_cot.shape, 0) % pad
+    packed[...] = jnp.where(kind == units, flat, turned_cot).astype(jnp.bfloat16)
+
+    @pl.loop(1, count)
+    def _(step):
+        piece(step).start()
+
+    mine = pl.ds(pl.multiple_of(me * pad, pad), pad)
+    own = pltpu.make_async_copy(packed.at[mine], landed.at[mine], own_sem.at[0])
+    own.start()
+
+    for h in range(1, groups):
+        along(h).wait_recv()
+        for q in range(1, pairs):
+            across(h, q).start()
+        sideways(h, 0).start()
+
+    for b in range(blocks):
+        loads[b].wait()
+        for c in range(2 * b * here, 2 * (b + 1) * here):
+            weights[c * experts : (c + 1) * experts, :] = held[
+                :, c * width : (c + 1) * width
+            ].astype(jnp.bfloat16)
+
+    for h in range(groups):
+        for q in range(1, pairs):
+            across(h, q).wait_recv()
+            sideways(h, q).start()
+
+    own.wait()
+
+    @pl.loop(1, count)
+    def _(step):
+        piece(step).wait()
+
+    from_row = lax.broadcasted_iota(jnp.int32, (own_rows * top, total), 0)
+    to_col = lax.broadcasted_iota(jnp.int32, (own_rows * top, total), 1) % own_rows
+    source_row = lax.broadcasted_iota(jnp.int32, (count * pad, total), 0) // pad
+    source_col = lax.broadcasted_iota(jnp.int32, (count * pad, total), 1) // own_rows
+    same = (source_row == source_col).astype(jnp.float32)
+    unit_row = lax.broadcasted_iota(jnp.int32, (pad, count * pad), 0)
+    unit_col = lax.broadcasted_iota(jnp.int32, (pad, count * pad), 1) % pad
+    gather = (unit_row == unit_col).astype(jnp.bfloat16)
+    for a in range(top):
+        lanes = (from_row == to_col * top + a).astype(jnp.bfloat16)
+        wide = jnp.dot(landed[...], lanes, preferred_element_type=jnp.float32) * same
+        turned[a] = jnp.dot(
+            gather, wide.astype(jnp.bfloat16), preferred_element_type=jnp.float32
+        )
+
+    for h in range(groups):
+        for q in range(pairs):
+            sideways(h, q).wait_recv()
+
+    expert_row = lax.broadcasted_iota(jnp.int32, (experts, total), 0).astype(jnp.float32)
+    for a in range(top):
+        names[a : a + 1, :] = turned[a, units : units + 1, :]
+
+    @pl.loop(0, blocks)
+    def _(b):
+        first = pl.multiple_of(b * (2 * here * experts), 2 * here * experts)
+        values = lax.dot_general(
+            weights[pl.ds(first, 2 * here * experts), :],
+            all_tokens[...],
+            NT,
+            preferred_element_type=jnp.float32,
+        )
+        hot = [(names[a : a + 1, :] == expert_row).astype(jnp.float32) for a in range(top)]
+        picked = []
+        both = []
+        for u in range(here):
+            gate = values[2 * u * experts : (2 * u + 1) * experts]
+            up = values[(2 * u + 1) * experts : (2 * u + 2) * experts]
+            cot_dense = turned[0, pl.ds(b * here + u, 1), :] * hot[0]
+            for a in range(1, top):
+                cot_dense = cot_dense + turned[a, pl.ds(b * here + u, 1), :] * hot[a]
+            sig = 1.0 / (1.0 + jnp.exp(-gate))
+            d_gate = cot_dense * up * (sig * (1.0 + gate * (1.0 - sig)))
+            d_up = cot_dense * (gate * sig)
+            both += [d_gate, d_up]
+            picked += [
+                jnp.sum(d * hot[a], axis=0, keepdims=True)
+                for d in (d_gate, d_up)
+                for a in range(top)
+            ]
+        dense[pl.ds(first, 2 * here * experts), :] = jnp.concatenate(both, axis=0).astype(
+            jnp.bfloat16
+        )
+        start = pl.multiple_of(member * (blocks * share) + b * share, share)
+        spread[pl.ds(start, share), :] = jnp.concatenate(picked, axis=0).astype(jnp.bfloat16)
+        for q in range(1, pairs):
+            swap(b, q).start()
+        pass_on(b, 0).start()
+
+        @pl.when(b > 0)
+        def _():
+            for q in range(1, pairs):
+                swap(b - 1, q).wait_recv()
+                pass_on(b - 1, q).start()
+
+    for q in range(1, pairs):
+        swap(blocks - 1, q).wait_recv()
+        pass_on(blocks - 1, q).start()
+
+    for h in range(groups):
+        if h:
+            along(h).wait_send()
+        for q in range(pairs):
+            if q:
+                across(h, q).wait_send()
+            sideways(h, q).wait_send()
+    for b in range(blocks):
+        for q in range(pairs):
+            if q:
+                swap(b, q).wait_send()
+            pass_on(b, q).wait()
+
+
+def exchange(units, tokens, cotangent, expert_ids, master):
+    groups, members = lax.axis_size("dp"), lax.axis_size("expert")
+    count = groups * members
+    own_rows, width = tokens.shape
+    top, hidden = cotangent.shape[1:]
+    total = own_rows * count
+    experts = master.shape[0]
+    pad = -(-(units + 1) // 16) * 16
+    blocks = block_count(units, 3)
+    dma = pltpu.SemaphoreType.DMA
+    vmem = pl.BlockSpec(memory_space=pltpu.VMEM)
+    return pl.pallas_call(
+        functools.partial(exchange_kernel, units, pad, blocks),
+        in_specs=[vmem, vmem, vmem, pl.BlockSpec(memory_space=pl.ANY)],
+        out_specs=[vmem] * 4,
+        out_shape=[
+            jax.ShapeDtypeStruct((total, width), jnp.bfloat16),
+            jax.ShapeDtypeStruct((2 * units * experts, total), jnp.bfloat16),
+            jax.ShapeDtypeStruct((members * 2 * units * top, total), jnp.bfloat16),
+            jax.ShapeDtypeStruct((top, total), jnp.float32),
+        ],
+        scratch_shapes=[
+            pltpu.VMEM(master.shape, jnp.float32),
+            pltpu.VMEM((2 * units * experts, width), jnp.bfloat16),
+            pltpu.VMEM((count * pad, own_rows * top), jnp.bfloat16),
+            pltpu.VMEM((count * pad, own_rows * top), jnp.bfloat16),
+            pltpu.VMEM((top, pad, total), jnp.float32),
+            dma((blocks,)),
+            dma((1,)),
+            dma((2, groups)),
+            dma((2, groups, members // 2)),
+            dma((2, groups, members // 2)),
+            dma((2, count)),
+            dma((2, blocks, members // 2)),
+            dma((2, blocks, members // 2)),
+        ],
+        compiler_params=pltpu.CompilerParams(
+            collective_id=0, has_side_effects=True, vmem_limit_bytes=VMEM_LIMIT
+        ),
+        name="exchange",
+    )(tokens, cotangent.reshape(own_rows * top, hidden), expert_ids, master)
+
+
+def finish_kernel(
+    top, mask, spread, dense, tokens, master, first, second,
+    new_master, new_first, new_second, out, fold,
+):
+    experts = master.shape[0]
+    width = tokens.shape[1]
+    units = out.shape[1]
+    rows = spread.shape[0]
+
+    @pl.when(pl.program_id(0) == 0)
+    def _():
+        out_row = lax.broadcasted_iota(jnp.int32, fold.shape, 0)
+        in_row = lax.broadcasted_iota(jnp.int32, fold.shape, 1) // top
+        wanted = (in_row % 2) * units + in_row // 2
+        fold[...] = (out_row == wanted).astype(jnp.bfloat16)
+
+    both = jnp.concatenate([mask[0], mask[0]], axis=0)
+    masked = spread[...].reshape(rows // (2 * top), 2 * top, -1) * both[None]
+    chosen = jnp.dot(
+        fold[...], masked.reshape(rows, -1), preferred_element_type=jnp.float32
+    ).astype(jnp.bfloat16)
+    grad = jnp.dot(chosen, tokens[...], preferred_element_type=jnp.float32)
+    out[0, :, :width] = grad[:units]
+    out[0, :, width:] = grad[units:]
+    grads = jnp.dot(dense[...], tokens[...], preferred_element_type=jnp.float32)
+    for c in range(master.shape[1] // width):
+        cols = slice(c * width, (c + 1) * width)
+        results = adamw_update(
+            master[:, cols],
+            first[:, cols],
+            second[:, cols],
+            grads[c * experts : (c + 1) * experts],
+        )
+        new_master[:, cols], new_first[:, cols], new_second[:, cols] = results
+
+
+def finish(units, top, mask, spread, dense, tokens, master, first, second):
+    slots, _, total = mask.shape
+    experts, shard = master.shape
+    width = tokens.shape[1]
+    state = pl.BlockSpec((experts, shard // slots), lambda i: (0, i))
+    return pl.pallas_call(
+        functools.partial(finish_kernel, top),
+        grid=(slots,),
+        in_specs=[
+            pl.BlockSpec((1, top, total), lambda i: (i, 0, 0)),
+            pl.BlockSpec(spread.shape, lambda i: (0, 0)),
+            pl.BlockSpec((dense.shape[0] // slots, total), lambda i: (i, 0)),
+            pl.BlockSpec(tokens.shape, lambda i: (0, 0)),
+            state,
+            state,
+            state,
+        ],
+        out_specs=[state] * 3 + [pl.BlockSpec((1, units, 2 * width), lambda i: (i, 0, 0))],
+        out_shape=[jax.ShapeDtypeStruct(master.shape, jnp.float32)] * 3
+        + [jax.ShapeDtypeStruct((slots, units, 2 * width), jnp.float32)],
+        scratch_shapes=[pltpu.VMEM((2 * units, spread.shape[0]), jnp.bfloat16)],
+        compiler_params=pltpu.CompilerParams(
+            dimension_semantics=("arbitrary",), vmem_limit_bytes=VMEM_LIMIT
+        ),
+        name="finish",
+    )(mask, spread, dense, tokens, master, first, second)
+
+
+def slot_masks(placement, names, slot_local, token_rows):
+    expert_devices = lax.axis_size("expert")
+    slot_count = placement.shape[0]
+    slot_range = jnp.arange(slot_count, dtype=jnp.int32)
+    same = placement[:, None] == placement[None, :]
+    replicas = jnp.sum(same.astype(jnp.int32), axis=1)
+    earlier = same & (slot_range[:, None] > slot_range[None, :])
+    rank = jnp.sum(earlier.astype(jnp.int32), axis=1)
+    first_slot = lax.axis_index("expert") * slot_local
+    own = lambda values: lax.dynamic_slice_in_dim(values, first_slot, slot_local)
+    source = jnp.arange(names.shape[1], dtype=jnp.int32) // token_rows % expert_devices
+    chosen = source[None, :] % own(replicas)[:, None] == own(rank)[:, None]
+    held = own(placement)[:, None, None].astype(names.dtype) == names[None]
+    return (held & chosen[:, None, :]).astype(jnp.bfloat16)
+
+
+def move_tokens(tokens, cotangent, expert_ids, placement, master, first_moment, second_moment):
+    members = lax.axis_size("expert")
+    top = cotangent.shape[1]
+    units = master.shape[1] // (2 * tokens.shape[1])
+    slot_local = placement.shape[0] // members
+    all_tokens, dense, spread, names = exchange(units, tokens, cotangent, expert_ids, master)
+    mask = slot_masks(placement, names, slot_local, tokens.shape[0])
+    return tuple(
+        finish(
+            units * members, top, mask, spread, dense, all_tokens,
+            master, first_moment, second_moment,
+        )
+    )
+
+
+def local(tokens, cotangent, expert_ids, placement, master, first_moment, second_moment):
+    devices = lax.axis_size("dp") * lax.axis_size("expert")
+    token_values = tokens.size * devices
+    weight_values = placement.shape[0] // lax.axis_size("expert") * cotangent.shape[2] * 2 * tokens.shape[1]
+    whole_units = master.shape[1] % (2 * tokens.shape[1]) == 0
+    few = token_values < weight_values and tokens.shape[0] * devices % 128 == 0
+    exact = master.shape[0] <= 256 and tokens.shape[0] % 16 == 0 and cotangent.shape[1] % 8 == 0
+    slot_local = placement.shape[0] // lax.axis_size("expert")
+    even = lax.axis_size("expert") % 2 == 0
+    even = even and master.shape[1] // tokens.shape[1] % slot_local == 0
+    plan = move_tokens if whole_units and few and exact and even else move_weights
+    return plan(tokens, cotangent, expert_ids, placement, master, first_moment, second_moment)
+
+
 def solution(mesh):
     return jax.shard_map(
         local,

time: 1180 us -> 72.8 us (0.06)
  waiting for transfers between devices: 879 us -> 0 us
  local copies, waits for them, and re-layouts: 135 us -> 1.44 us
  blocking collectives: 76.5 us -> 0 us
  Pallas kernels: 0 us -> 66.9 us
  matrix products: 38.1 us -> 0 us
  between operations: 14.7 us -> 0.65 us
  starting transfers between devices: 12.9 us -> 0 us
    reduce_scatter x1 -> x0, waiting for transfers between devices: 413 us -> none  [local(): lax.psum_scatter(grad_block.reshape(lax.axis_size('dp') * piece_rows, slo...]
    all_gather x1 -> x0, waiting for transfers between devices: 403 us -> none  [local(): replica = lax.all_gather(own_piece, 'dp', axis=1, tiled=True)]
    all_to_all x1 -> x0, blocking collectives: 76.5 us -> none  [local(): lax.all_to_all(send_weight, 'expert', split_axis=1, concat_axis=1, tiled=...]
    pallas_call x0 -> x2, Pallas kernels: none -> 66.9 us  [the longest x1 42.8 us: exchange(): pl.pallas_call(functools.partial(exchange_kernel, units, pad, blocks), in...]
    all_to_all x3 -> x0, waiting for transfers between devices: 63.6 us -> none  [the longest x1 62.3 us: local(): lax.all_to_all(outgoing.astype(jnp.bfloat16), 'expert', split_axis=1, con...]
    convert_element_type x4 -> x0, local copies, waits for them, and re-layouts: 58.4 us -> none  [the longest x1 30.7 us: local(): grad_block.reshape(lax.axis_size('dp') * piece_rows, slot_local, 2 * mode...]
    dot_general x3 -> x0, matrix products: 38.1 us -> none  [the longest x1 15.9 us: local(): jnp.dot(slot_hot.T.astype(jnp.float32), by_slot, precision=lax.Precision....]
    all_gather x1 -> x0, local copies, waits for them, and re-layouts: 32.6 us -> none  [local(): replica = lax.all_gather(own_piece, 'dp', axis=1, tiled=True)]
  transfers between devices with their start and end apart: 5 -> 0, of which waited for: 4 -> 0; matrix products, arithmetic and copies ran while one was open for 5% -> 0% of each run, Pallas kernels for 0% -> 0%
where the time goes in v2:
time: 72.8 us; the launch traced here: 72.4 us
  Pallas kernels  66.9 us (92%)
  other arithmetic  3.42 us (5%)
  local copies, waits for them, and re-layouts  1.44 us (2%)
    pallas_call x1, Pallas kernels, exchange(): pl.pallas_call(functools.partial(exchange_kernel, units, pad, blocks), in...  42.8 us
    pallas_call x1, Pallas kernels, finish(): pl.pallas_call(functools.partial(finish_kernel, top), grid=(slots,), in_s...  24.1 us

profile of v2, /device:TPU:0, one launch (start us, length us, event | category | flops | bytes accessed | tf_op | source)
XLA Modules:
  0.0 72.4 jit_solution(3648691272800275071)
XLA Ops:
  0.6 0.7 %dynamic-slice_convert_fusion = f32[8]{0:T(128)S(1)} fusion(s32[64]{0:T(128)} %param.10, s32[]{:T(128)S(6)} %select_n.39), kind=kLoop, calls=%fused_computation.25 | loop fusion | flops 8 | bytes 68 | tf_op jit(solution)/shard_map/convert_element_type | solution.py:475
  1.4 0.9 %fusion = (s32[64]{0:T(128)S(1)}, s32[64]{0:T(128)S(1)}) fusion(s32[64]{0:T(128)} %param.10), kind=kLoop, calls=%fused_computation.7 | loop fusion | flops 28544 | bytes 768 | tf_op jit(solution)/shard_map/reduce_sum | solution.py:468
  2.3 0.1 dynamic_slice.11
  2.4 0.1 broadcast_compare_fusion
  2.4 0.3 fusion.1
  2.7 1.4 %copy.12.ids = s32[16,8]{1,0:T(8,128)} copy(s32[16,8]{0,1:T(8,128)} %param.9) | data formatting | bytes 1024 | tf_op args[2]
  4.1 42.8 %exchange.1 = (bf16[512,2048]{1,0:T(8,128)(2,1)}, bf16[768,512]{1,0:T(8,128)(2,1)}, bf16[1536,512]{1,0:T(8,128)(2,1)}, f32[8,512]{1,0:T(8,128)}) custom-call(bf16[16,2048]{1,0:T(8,128)(2,1)} %tokens.1, bf16[128,384]{1,0:T(8,128)(2,1)} %bitcast.1, s32[16,8]{1,0:T(8,128)} %copy.12.ids, f32[32,49152]{1,0:T(8,128)} %master.3), custom_call_target="tpu_custom_call" | custom-call | tf_op jit(solution)/shard_map/exchange/pallas_call | solution.py:367
  46.9 1.4 %and_convert_fusion.mask = bf16[8,8,512]{2,1,0:T(8,128)(2,1)} fusion(f32[8,512]{1,0:T(8,128)} %get-tuple-element.8, f32[8]{0:T(128)S(1)} %dynamic-slice_convert_fusion, pred[8,512]{1,0:T(8,128)(4,1)S(1)} %fusion.1), kind=kLoop, calls=%fused_computation | loop fusion | flops 98304 | bytes 86048 | tf_op jit(solution)/shard_map/convert_element_type | solution.py:476
  48.3 24.1 %finish.1 = (f32[32,49152]{1,0:T(8,128)}, f32[32,49152]{1,0:T(8,128)}, f32[32,49152]{1,0:T(8,128)}, f32[8,96,4096]{2,1,0:T(8,128)}) custom-call(bf16[8,8,512]{2,1,0:T(8,128)(2,1)} %and_convert_fusion.mask, bf16[1536,512]{1,0:T(8,128)(2,1)} %get-tuple-element.9.spread, bf16[768,512]{1,0:T(8,128)(2,1)} %get-tuple-element.10.dense, ...), custom_call_target="tpu_custom_call" | custom-call | tf_op jit(solution)/shard_map/finish/pallas_call | solution.py:440
  (1 shorter events, 0.0 us)

commit v3 on v2

--- a/solution.py
+++ b/solution.py
@@ -135,7 +135,7 @@
 def exchange_kernel(
     units, pad, blocks, tokens, cot, ids, master,
     all_tokens, dense, spread, names,
-    held, weights, packed, landed, turned,
+    held, weights, packed, landed,
     held_sem, own_sem, row_sems, plane_sems, pair_sems, piece_sems, swap_sems, share_sems,
 ):
     groups, members = lax.axis_size("dp"), lax.axis_size("expert")
@@ -145,9 +145,9 @@
     pair, half = member // 2, member % 2
     me = group * members + member
     own_rows, width = tokens.shape
-    experts, top = master.shape[0], ids.shape[1]
-    total = all_tokens.shape[0]
+    experts, top = master.shape[0], ids.shape[0]
     here = units // blocks
+    group_rows = members * own_rows
     block_cols = master.shape[1] // blocks
 
     def device(g, e):
@@ -182,20 +182,20 @@
         target = landed.at[pl.ds(pl.multiple_of(me * pad, pad), pad)]
         return remote(source, target, piece_sems, (step,), device(other // members, other % members))
 
-    share = 2 * here * top
-
-    def part(b, q, c):
+    share = 2 * units * top
+
+    def part(h, q, c):
         owner = 2 * ((pair + pairs - q) % pairs) + c
-        start = owner * (blocks * share) + b * share
-        return spread.at[pl.ds(pl.multiple_of(start, share), share)]
-
-    def swap(b, q):
+        rows = pl.ds(pl.multiple_of(owner * share, share), share)
+        return spread.at[(group + groups - h) % groups, rows]
+
+    def swap(h, q):
         to = device(group, 2 * ((pair + q) % pairs) + half)
-        return remote(part(b, 0, half), part(b, 0, half), swap_sems, (b, q), to)
-
-    def pass_on(b, q):
+        return remote(part(h, 0, half), part(h, 0, half), swap_sems, (h, q), to)
+
+    def pass_on(h, q):
         to = device(group, 2 * pair + 1 - half)
-        return remote(part(b, q, half), part(b, q, half), share_sems, (b, q), to)
+        return remote(part(h, q, half), part(h, q, half), share_sems, (h, q), to)
 
     loads = []
     for b in range(blocks):
@@ -228,12 +228,12 @@
     wanted = (out_row // pad) * units + out_row % pad
     pick = ((in_col == wanted) & (out_row % pad < units)).astype(jnp.bfloat16)
     turned_cot = lax.dot_general(pick, cot[...], NT, preferred_element_type=jnp.float32)
-    lane = lax.broadcasted_iota(jnp.int32, (own_rows, own_rows * top), 1)
-    row = lax.broadcasted_iota(jnp.int32, (own_rows, own_rows * top), 0)
-    flat = jnp.zeros((own_rows, own_rows * top), jnp.float32)
+    lane = lax.broadcasted_iota(jnp.int32, (top, own_rows * top), 1)
+    row = lax.broadcasted_iota(jnp.int32, (top, own_rows * top), 0)
+    flat = jnp.zeros((top, own_rows * top), jnp.float32)
     numbers = ids[...].astype(jnp.float32)
-    for a in range(top):
-        flat = flat + jnp.where(lane == row * top + a, numbers[:, a : a + 1], 0.0)
+    for t in range(own_rows):
+        flat = flat + jnp.where(lane == t * top + row, numbers[:, t : t + 1], 0.0)
     flat = jnp.sum(flat, axis=0, keepdims=True)
     kind = lax.broadcasted_iota(jnp.int32, turned_cot.shape, 0) % pad
     packed[...] = jnp.where(kind == units, flat, turned_cot).astype(jnp.bfloat16)
@@ -259,85 +259,94 @@
                 :, c * width : (c + 1) * width
             ].astype(jnp.bfloat16)
 
-    for h in range(groups):
+    own.wait()
+
+    from_row = lax.broadcasted_iota(jnp.int32, (own_rows * top, group_rows), 0)
+    to_col = lax.broadcasted_iota(jnp.int32, (own_rows * top, group_rows), 1) % own_rows
+    source_row = lax.broadcasted_iota(jnp.int32, (members * pad, group_rows), 0) // pad
+    source_col = lax.broadcasted_iota(jnp.int32, (members * pad, group_rows), 1) // own_rows
+    same = (source_row == source_col).astype(jnp.float32)
+    unit_row = lax.broadcasted_iota(jnp.int32, (pad, members * pad), 0)
+    unit_col = lax.broadcasted_iota(jnp.int32, (pad, members * pad), 1) % pad
+    gather = (unit_row == unit_col).astype(jnp.bfloat16)
+    expert_row = lax.broadcasted_iota(jnp.int32, (experts, group_rows), 0).astype(jnp.float32)
+
+    @pl.loop(0, groups)
+    def _(h):
+        now = (group + groups - h) % groups
         for q in range(1, pairs):
             across(h, q).wait_recv()
             sideways(h, q).start()
-
-    own.wait()
+        for k in range(members):
+            step = (me + count - (now * members + k)) % count
+
+            @pl.when(step > 0)
+            def _():
+                piece(step).wait_recv()
+
+        pieces = landed[pl.ds(pl.multiple_of(now * members * pad, members * pad), members * pad), :]
+        turned = []
+        for a in range(top):
+            lanes = (from_row == to_col * top + a).astype(jnp.bfloat16)
+            wide = jnp.dot(pieces, lanes, preferred_element_type=jnp.float32) * same
+            turned.append(
+                jnp.dot(gather, wide.astype(jnp.bfloat16), preferred_element_type=jnp.float32)
+            )
+        columns = pl.ds(pl.multiple_of(now * group_rows, group_rows), group_rows)
+        names[:, columns] = jnp.concatenate([t[units : units + 1] for t in turned], axis=0)
+        hot = [(t[units : units + 1] == expert_row).astype(jnp.float32) for t in turned]
+
+        for q in range(pairs):
+            sideways(h, q).wait_recv()
+        group_tokens = all_tokens[columns, :]
+        picked = []
+        for b in range(blocks):
+            first = b * (2 * here * experts)
+            values = lax.dot_general(
+                weights[first : first + 2 * here * experts, :],
+                group_tokens,
+                NT,
+                preferred_element_type=jnp.float32,
+            )
+            both = []
+            for u in range(here):
+                gate = values[2 * u * experts : (2 * u + 1) * experts]
+                up = values[(2 * u + 1) * experts : (2 * u + 2) * experts]
+                unit = b * here + u
+                cot_dense = turned[0][unit : unit + 1] * hot[0]
+                for a in range(1, top):
+                    cot_dense = cot_dense + turned[a][unit : unit + 1] * hot[a]
+                sig = 1.0 / (1.0 + jnp.exp(-gate))
+                d_gate = cot_dense * up * (sig * (1.0 + gate * (1.0 - sig)))
+                d_up = cot_dense * (gate * sig)
+                both += [d_gate, d_up]
+                picked += [
+                    jnp.sum(d * hot[a], axis=0, keepdims=True)
+                    for d in (d_gate, d_up)
+                    for a in range(top)
+                ]
+            dense[first : first + 2 * here * experts, columns] = jnp.concatenate(
+                both, axis=0
+            ).astype(jnp.bfloat16)
+        rows = pl.ds(pl.multiple_of(member * share, share), share)
+        spread[now, rows, :] = jnp.concatenate(picked, axis=0).astype(jnp.bfloat16)
+        for q in range(1, pairs):
+            swap(h, q).start()
+        pass_on(h, 0).start()
+
+        @pl.when(h > 0)
+        def _():
+            for q in range(1, pairs):
+                swap(h - 1, q).wait_recv()
+                pass_on(h - 1, q).start()
+
+    for q in range(1, pairs):
+        swap(groups - 1, q).wait_recv()
+        pass_on(groups - 1, q).start()
 
     @pl.loop(1, count)
     def _(step):
-        piece(step).wait()
-
-    from_row = lax.broadcasted_iota(jnp.int32, (own_rows * top, total), 0)
-    to_col = lax.broadcasted_iota(jnp.int32, (own_rows * top, total), 1) % own_rows
-    source_row = lax.broadcasted_iota(jnp.int32, (count * pad, total), 0) // pad
-    source_col = lax.broadcasted_iota(jnp.int32, (count * pad, total), 1) // own_rows
-    same = (source_row == source_col).astype(jnp.float32)
-    unit_row = lax.broadcasted_iota(jnp.int32, (pad, count * pad), 0)
-    unit_col = lax.broadcasted_iota(jnp.int32, (pad, count * pad), 1) % pad
-    gather = (unit_row == unit_col).astype(jnp.bfloat16)
-    for a in range(top):
-        lanes = (from_row == to_col * top + a).astype(jnp.bfloat16)
-        wide = jnp.dot(landed[...], lanes, preferred_element_type=jnp.float32) * same
-        turned[a] = jnp.dot(
-            gather, wide.astype(jnp.bfloat16), preferred_element_type=jnp.float32
-        )
-
-    for h in range(groups):
-        for q in range(pairs):
-            sideways(h, q).wait_recv()
-
-    expert_row = lax.broadcasted_iota(jnp.int32, (experts, total), 0).astype(jnp.float32)
-    for a in range(top):
-        names[a : a + 1, :] = turned[a, units : units + 1, :]
-
-    @pl.loop(0, blocks)
-    def _(b):
-        first = pl.multiple_of(b * (2 * here * experts), 2 * here * experts)
-        values = lax.dot_general(
-            weights[pl.ds(first, 2 * here * experts), :],
-            all_tokens[...],
-            NT,
-            preferred_element_type=jnp.float32,
-        )
-        hot = [(names[a : a + 1, :] == expert_row).astype(jnp.float32) for a in range(top)]
-        picked = []
-        both = []
-        for u in range(here):
-            gate = values[2 * u * experts : (2 * u + 1) * experts]
-            up = values[(2 * u + 1) * experts : (2 * u + 2) * experts]
-            cot_dense = turned[0, pl.ds(b * here + u, 1), :] * hot[0]
-            for a in range(1, top):
-                cot_dense = cot_dense + turned[a, pl.ds(b * here + u, 1), :] * hot[a]
-            sig = 1.0 / (1.0 + jnp.exp(-gate))
-            d_gate = cot_dense * up * (sig * (1.0 + gate * (1.0 - sig)))
-            d_up = cot_dense * (gate * sig)
-            both += [d_gate, d_up]
-            picked += [
-                jnp.sum(d * hot[a], axis=0, keepdims=True)
-                for d in (d_gate, d_up)
-                for a in range(top)
-            ]
-        dense[pl.ds(first, 2 * here * experts), :] = jnp.concatenate(both, axis=0).astype(
-            jnp.bfloat16
-        )
-        start = pl.multiple_of(member * (blocks * share) + b * share, share)
-        spread[pl.ds(start, share), :] = jnp.concatenate(picked, axis=0).astype(jnp.bfloat16)
-        for q in range(1, pairs):
-            swap(b, q).start()
-        pass_on(b, 0).start()
-
-        @pl.when(b > 0)
-        def _():
-            for q in range(1, pairs):
-                swap(b - 1, q).wait_recv()
-                pass_on(b - 1, q).start()
-
-    for q in range(1, pairs):
-        swap(blocks - 1, q).wait_recv()
-        pass_on(blocks - 1, q).start()
+        piece(step).wait_send()
 
     for h in range(groups):
         if h:
@@ -345,12 +354,9 @@
         for q in range(pairs):
             if q:
                 across(h, q).wait_send()
+                swap(h, q).wait_send()
             sideways(h, q).wait_send()
-    for b in range(blocks):
-        for q in range(pairs):
-            if q:
-                swap(b, q).wait_send()
-            pass_on(b, q).wait()
+            pass_on(h, q).wait()
 
 
 def exchange(units, tokens, cotangent, expert_ids, master):
@@ -371,7 +377,7 @@
         out_shape=[
             jax.ShapeDtypeStruct((total, width), jnp.bfloat16),
             jax.ShapeDtypeStruct((2 * units * experts, total), jnp.bfloat16),
-            jax.ShapeDtypeStruct((members * 2 * units * top, total), jnp.bfloat16),
+            jax.ShapeDtypeStruct((groups, members * 2 * units * top, members * own_rows), jnp.bfloat16),
             jax.ShapeDtypeStruct((top, total), jnp.float32),
         ],
         scratch_shapes=[
@@ -379,31 +385,30 @@
             pltpu.VMEM((2 * units * experts, width), jnp.bfloat16),
             pltpu.VMEM((count * pad, own_rows * top), jnp.bfloat16),
             pltpu.VMEM((count * pad, own_rows * top), jnp.bfloat16),
-            pltpu.VMEM((top, pad, total), jnp.float32),
             dma((blocks,)),
             dma((1,)),
             dma((2, groups)),
             dma((2, groups, members // 2)),
             dma((2, groups, members // 2)),
             dma((2, count)),
-            dma((2, blocks, members // 2)),
-            dma((2, blocks, members // 2)),
+            dma((2, groups, members // 2)),
+            dma((2, groups, members // 2)),
         ],
         compiler_params=pltpu.CompilerParams(
             collective_id=0, has_side_effects=True, vmem_limit_bytes=VMEM_LIMIT
         ),
         name="exchange",
-    )(tokens, cotangent.reshape(own_rows * top, hidden), expert_ids, master)
+    )(tokens, cotangent.reshape(own_rows * top, hidden), expert_ids.T, master)
 
 
 def finish_kernel(
-    top, mask, spread, dense, tokens, master, first, second,
+    top, token_rows, placement, names, spread, dense, tokens, master, first, second,
     new_master, new_first, new_second, out, fold,
 ):
     experts = master.shape[0]
     width = tokens.shape[1]
     units = out.shape[1]
-    rows = spread.shape[0]
+    groups, rows, group_rows = spread.shape
 
     @pl.when(pl.program_id(0) == 0)
     def _():
@@ -412,10 +417,31 @@
         wanted = (in_row % 2) * units + in_row // 2
         fold[...] = (out_row == wanted).astype(jnp.bfloat16)
 
-    both = jnp.concatenate([mask[0], mask[0]], axis=0)
-    masked = spread[...].reshape(rows // (2 * top), 2 * top, -1) * both[None]
+    slot = lax.axis_index("expert") * pl.num_programs(0) + pl.program_id(0)
+    expert = placement[slot]
+    replicas, rank = jnp.int32(0), jnp.int32(0)
+    for other in range(placement.shape[0]):
+        equal = jnp.where(placement[other] == expert, 1, 0)
+        replicas = replicas + equal
+        rank = rank + jnp.where(other < slot, equal, 0)
+    lane = lax.broadcasted_iota(jnp.int32, names.shape, 1)
+    source = (lane // token_rows) % lax.axis_size("expert")
+    chosen_source = lax.rem(source, jnp.full(source.shape, replicas)) == rank
+    held = names[...] == expert.astype(jnp.float32)
+    mask = jnp.where(held & chosen_source, 1.0, 0.0)
+    both = jnp.concatenate([mask, mask], axis=0).astype(jnp.bfloat16)
+    masked = jnp.concatenate(
+        [
+            (
+                spread[g].reshape(rows // (2 * top), 2 * top, group_rows)
+                * both[None, :, g * group_rows : (g + 1) * group_rows]
+            ).reshape(rows, group_rows)
+            for g in range(groups)
+        ],
+        axis=1,
+    )
     chosen = jnp.dot(
-        fold[...], masked.reshape(rows, -1), preferred_element_type=jnp.float32
+        fold[...], masked, preferred_element_type=jnp.float32
     ).astype(jnp.bfloat16)
     grad = jnp.dot(chosen, tokens[...], preferred_element_type=jnp.float32)
     out[0, :, :width] = grad[:units]
@@ -432,17 +458,18 @@
         new_master[:, cols], new_first[:, cols], new_second[:, cols] = results
 
 
-def finish(units, top, mask, spread, dense, tokens, master, first, second):
-    slots, _, total = mask.shape
+def finish(units, slots, token_rows, placement, names, spread, dense, tokens, master, first, second):
+    top, total = names.shape
     experts, shard = master.shape
     width = tokens.shape[1]
     state = pl.BlockSpec((experts, shard // slots), lambda i: (0, i))
     return pl.pallas_call(
-        functools.partial(finish_kernel, top),
+        functools.partial(finish_kernel, top, token_rows),
         grid=(slots,),
         in_specs=[
-            pl.BlockSpec((1, top, total), lambda i: (i, 0, 0)),
-            pl.BlockSpec(spread.shape, lambda i: (0, 0)),
+            pl.BlockSpec(memory_space=pltpu.SMEM),
+            pl.BlockSpec(names.shape, lambda i: (0, 0)),
+            pl.BlockSpec(spread.shape, lambda i: (0, 0, 0)),
             pl.BlockSpec((dense.shape[0] // slots, total), lambda i: (i, 0)),
             pl.BlockSpec(tokens.shape, lambda i: (0, 0)),
             state,
@@ -452,40 +479,22 @@
         out_specs=[state] * 3 + [pl.BlockSpec((1, units, 2 * width), lambda i: (i, 0, 0))],
         out_shape=[jax.ShapeDtypeStruct(master.shape, jnp.float32)] * 3
         + [jax.ShapeDtypeStruct((slots, units, 2 * width), jnp.float32)],
-        scratch_shapes=[pltpu.VMEM((2 * units, spread.shape[0]), jnp.bfloat16)],
+        scratch_shapes=[pltpu.VMEM((2 * units, spread.shape[1]), jnp.bfloat16)],
         compiler_params=pltpu.CompilerParams(
             dimension_semantics=("arbitrary",), vmem_limit_bytes=VMEM_LIMIT
         ),
         name="finish",
-    )(mask, spread, dense, tokens, master, first, second)
-
-
-def slot_masks(placement, names, slot_local, token_rows):
-    expert_devices = lax.axis_size("expert")
-    slot_count = placement.shape[0]
-    slot_range = jnp.arange(slot_count, dtype=jnp.int32)
-    same = placement[:, None] == placement[None, :]
-    replicas = jnp.sum(same.astype(jnp.int32), axis=1)
-    earlier = same & (slot_range[:, None] > slot_range[None, :])
-    rank = jnp.sum(earlier.astype(jnp.int32), axis=1)
-    first_slot = lax.axis_index("expert") * slot_local
-    own = lambda values: lax.dynamic_slice_in_dim(values, first_slot, slot_local)
-    source = jnp.arange(names.shape[1], dtype=jnp.int32) // token_rows % expert_devices
-    chosen = source[None, :] % own(replicas)[:, None] == own(rank)[:, None]
-    held = own(placement)[:, None, None].astype(names.dtype) == names[None]
-    return (held & chosen[:, None, :]).astype(jnp.bfloat16)
+    )(placement, names, spread, dense, tokens, master, first, second)
 
 
 def move_tokens(tokens, cotangent, expert_ids, placement, master, first_moment, second_moment):
     members = lax.axis_size("expert")
-    top = cotangent.shape[1]
     units = master.shape[1] // (2 * tokens.shape[1])
     slot_local = placement.shape[0] // members
     all_tokens, dense, spread, names = exchange(units, tokens, cotangent, expert_ids, master)
-    mask = slot_masks(placement, names, slot_local, tokens.shape[0])
     return tuple(
         finish(
-            units * members, top, mask, spread, dense, all_tokens,
+            units * members, slot_local, tokens.shape[0], placement, names, spread, dense, all_tokens,
             master, first_moment, second_moment,
         )
     )
@@ -496,7 +505,7 @@
     token_values = tokens.size * devices
     weight_values = placement.shape[0] // lax.axis_size("expert") * cotangent.shape[2] * 2 * tokens.shape[1]
     whole_units = master.shape[1] % (2 * tokens.shape[1]) == 0
-    few = token_values < weight_values and tokens.shape[0] * devices % 128 == 0
+    few = token_values < weight_values and tokens.shape[0] * lax.axis_size("expert") % 128 == 0
     exact = master.shape[0] <= 256 and tokens.shape[0] % 16 == 0 and cotangent.shape[1] % 8 == 0
     slot_local = placement.shape[0] // lax.axis_size("expert")
     even = lax.axis_size("expert") % 2 == 0

time: 72.8 us -> 64.8 us (0.89)
  other arithmetic: 3.42 us -> 0 us
  Pallas kernels: 66.9 us -> 63.9 us
  local copies, waits for them, and re-layouts: 1.44 us -> 0 us
    pallas_call x1, Pallas kernels: 42.8 us -> 40.1 us  [exchange(): pl.pallas_call(functools.partial(exchange_kernel, units, pad, blocks), in...]
    convert_element_type x2 -> x0, other arithmetic: 2.15 us -> none  [the longest x1 1.42 us: slot_masks(): return (held & chosen[:, None, :]).astype(jnp.bfloat16)]
    unnamed x1 -> x0, local copies, waits for them, and re-layouts: 1.36 us -> none
    reduce_sum x1 -> x0, other arithmetic: 0.91 us -> none  [slot_masks(): replicas = jnp.sum(same.astype(jnp.int32), axis=1)]
where the time goes in v3:
time: 64.8 us; the launch traced here: 64.5 us
  Pallas kernels  63.9 us (99%)
    pallas_call x1, Pallas kernels, exchange(): pl.pallas_call(functools.partial(exchange_kernel, units, pad, blocks), in...  40.1 us
    pallas_call x1, Pallas kernels, finish(): pl.pallas_call(functools.partial(finish_kernel, top, token_rows), grid=(s...  23.7 us

profile of v3, /device:TPU:0, one launch (start us, length us, event | category | flops | bytes accessed | tf_op | source)
XLA Modules:
  0.0 64.5 jit_solution(18089086509769489704)
XLA Ops:
  0.6 40.1 %exchange.1 = (bf16[512,2048]{1,0:T(8,128)(2,1)}, bf16[768,512]{1,0:T(8,128)(2,1)}, bf16[4,1536,128]{2,1,0:T(8,128)(2,1)}, f32[8,512]{1,0:T(8,128)}) custom-call(bf16[16,2048]{1,0:T(8,128)(2,1)} %tokens.1, bf16[128,384]{1,0:T(8,128)(2,1)} %bitcast.2, s32[8,16]{1,0:T(8,128)} %bitcast.3, f32[32,49152]{1,0:T(8,128)} %master.3), custom_call_target="tpu_custom_call" | custom-call | tf_op jit(solution)/shard_map/exchange/pallas_call | solution.py:373
  40.8 23.7 %finish.1 = (f32[32,49152]{1,0:T(8,128)}, f32[32,49152]{1,0:T(8,128)}, f32[32,49152]{1,0:T(8,128)}, f32[8,96,4096]{2,1,0:T(8,128)}) custom-call(s32[64]{0:T(128)} %placement.1, f32[8,512]{1,0:T(8,128)} %get-tuple-element.8.names, bf16[4,1536,128]{2,1,0:T(8,128)(2,1)} %get-tuple-element.9.spread, bf16[768,512]{1,0:T(8,128)(2,1)} %get-tuple-element.10.dense, ...), custom_call_target="tpu_custom_call" | custom-call | tf_op jit(solution)/shard_map/finish/pallas_call | solution.py:466

commit v4 on v3

--- a/solution.py
+++ b/solution.py
@@ -160,8 +160,17 @@
             device_id=to, device_id_type=pl.DeviceIdType.MESH,
         )
 
+    relays = pairs == 4
+    direct = [q for q in range(1, pairs) if not (relays and q == 2)]
+
+    def order(place):
+        return place + (place // 2) * (1 - 2 * (place % 2)) if relays else place
+
+    def pair_at(offset):
+        return order((order(pair) + offset) % pairs)
+
     def shard(h, q, c):
-        owner = ((group + groups - h) % groups) * members + 2 * ((pair + pairs - q) % pairs) + c
+        owner = ((group + groups - h) % groups) * members + 2 * pair_at(pairs - q) + c
         return all_tokens.at[pl.ds(pl.multiple_of(owner * own_rows, own_rows), own_rows)]
 
     def along(h):
@@ -169,8 +178,21 @@
         return remote(shard(0, 0, half), shard(0, 0, half), row_sems, (h,), to)
 
     def across(h, q):
-        to = device(group, 2 * ((pair + q) % pairs) + half)
+        to = device(group, 2 * pair_at(q) + half)
         return remote(shard(h, 0, half), shard(h, 0, half), plane_sems, (h, q), to)
+
+    def relay(h):
+        via = 1 + 2 * (h % 2)
+        to = device(group, 2 * pair_at(via) + half)
+        return remote(shard(h, via, half), shard(h, via, half), plane_sems, (h, 2), to)
+
+    def arrived(h):
+        for q in direct:
+            across(h, q).wait_recv()
+        if relays:
+            relay(h).start()
+        for q in direct:
+            sideways(h, q).start()
 
     def sideways(h, q):
         to = device(group, 2 * pair + 1 - half)
@@ -185,13 +207,31 @@
     share = 2 * units * top
 
     def part(h, q, c):
-        owner = 2 * ((pair + pairs - q) % pairs) + c
+        owner = 2 * pair_at(pairs - q) + c
         rows = pl.ds(pl.multiple_of(owner * share, share), share)
         return spread.at[(group + groups - h) % groups, rows]
 
     def swap(h, q):
-        to = device(group, 2 * ((pair + q) % pairs) + half)
+        to = device(group, 2 * pair_at(q) + half)
         return remote(part(h, 0, half), part(h, 0, half), swap_sems, (h, q), to)
+
+    def swap_relay(h):
+        via = 1 + 2 * (h % 2)
+        to = device(group, 2 * pair_at(via) + half)
+        return remote(part(h, via, half), part(h, via, half), swap_sems, (h, 2), to)
+
+    def swapped(h):
+        for q in direct:
+            swap(h, q).wait_recv()
+        if relays:
+            swap_relay(h).start()
+        for q in direct:
+            pass_on(h, q).start()
+
+    def swapped_far(h):
+        if relays:
+            swap(h, 2).wait_recv()
+            pass_on(h, 2).start()
 
     def pass_on(h, q):
         to = device(group, 2 * pair + 1 - half)
@@ -219,7 +259,7 @@
 
     for h in range(1, groups):
         along(h).start()
-    for q in range(1, pairs):
+    for q in direct:
         across(0, q).start()
     sideways(0, 0).start()
 
@@ -248,10 +288,11 @@
 
     for h in range(1, groups):
         along(h).wait_recv()
-        for q in range(1, pairs):
+        for q in direct:
             across(h, q).start()
         sideways(h, 0).start()
 
+    arrived(0)
     for b in range(blocks):
         loads[b].wait()
         for c in range(2 * b * here, 2 * (b + 1) * here):
@@ -274,9 +315,14 @@
     @pl.loop(0, groups)
     def _(h):
         now = (group + groups - h) % groups
-        for q in range(1, pairs):
-            across(h, q).wait_recv()
-            sideways(h, q).start()
+        if relays:
+            across(h, 2).wait_recv()
+            sideways(h, 2).start()
+
+        @pl.when(h < groups - 1)
+        def _():
+            arrived(h + 1)
+
         for k in range(members):
             step = (me + count - (now * members + k)) % count
 
@@ -330,19 +376,21 @@
             ).astype(jnp.bfloat16)
         rows = pl.ds(pl.multiple_of(member * share, share), share)
         spread[now, rows, :] = jnp.concatenate(picked, axis=0).astype(jnp.bfloat16)
-        for q in range(1, pairs):
+        for q in direct:
             swap(h, q).start()
         pass_on(h, 0).start()
 
         @pl.when(h > 0)
         def _():
-            for q in range(1, pairs):
-                swap(h - 1, q).wait_recv()
-                pass_on(h - 1, q).start()
-
-    for q in range(1, pairs):
-        swap(groups - 1, q).wait_recv()
-        pass_on(groups - 1, q).start()
+            swapped(h - 1)
+
+        @pl.when(h > 1)
+        def _():
+            swapped_far(h - 2)
+
+    swapped(groups - 1)
+    for h in range(max(groups - 2, 0), groups):
+        swapped_far(h)
 
     @pl.loop(1, count)
     def _(step):
@@ -352,9 +400,12 @@
         if h:
             along(h).wait_send()
         for q in range(pairs):
-            if q:
+            if q in direct:
                 across(h, q).wait_send()
                 swap(h, q).wait_send()
+            elif q:
+                relay(h).wait_send()
+                swap_relay(h).wait_send()
             sideways(h, q).wait_send()
             pass_on(h, q).wait()
 

time: 64.8 us -> 68.6 us (1.059)
  Pallas kernels: 63.9 us -> 67.7 us
    pallas_call x1, Pallas kernels: 40.1 us -> 43.9 us  [exchange(): pl.pallas_call(functools.partial(exchange_kernel, units, pad, blocks), in...]
where the time goes in v4:
time: 68.6 us; the launch traced here: 68.3 us
  Pallas kernels  67.7 us (99%)
    pallas_call x1, Pallas kernels, exchange(): pl.pallas_call(functools.partial(exchange_kernel, units, pad, blocks), in...  43.9 us
    pallas_call x1, Pallas kernels, finish(): pl.pallas_call(functools.partial(finish_kernel, top, token_rows), grid=(s...  23.7 us

profile of v4, /device:TPU:0, one launch (start us, length us, event | category | flops | bytes accessed | tf_op | source)
XLA Modules:
  0.0 68.3 jit_solution(10662682199082267839)
XLA Ops:
  0.6 43.9 %exchange.1 = (bf16[512,2048]{1,0:T(8,128)(2,1)}, bf16[768,512]{1,0:T(8,128)(2,1)}, bf16[4,1536,128]{2,1,0:T(8,128)(2,1)}, f32[8,512]{1,0:T(8,128)}) custom-call(bf16[16,2048]{1,0:T(8,128)(2,1)} %tokens.1, bf16[128,384]{1,0:T(8,128)(2,1)} %bitcast.2, s32[8,16]{1,0:T(8,128)} %bitcast.3, f32[32,49152]{1,0:T(8,128)} %master.3), custom_call_target="tpu_custom_call" | custom-call | tf_op jit(solution)/shard_map/exchange/pallas_call | solution.py:424
  44.6 23.7 %finish.1 = (f32[32,49152]{1,0:T(8,128)}, f32[32,49152]{1,0:T(8,128)}, f32[32,49152]{1,0:T(8,128)}, f32[8,96,4096]{2,1,0:T(8,128)}) custom-call(s32[64]{0:T(128)} %placement.1, f32[8,512]{1,0:T(8,128)} %get-tuple-element.8.names, bf16[4,1536,128]{2,1,0:T(8,128)(2,1)} %get-tuple-element.9.spread, bf16[768,512]{1,0:T(8,128)(2,1)} %get-tuple-element.10.dense, ...), custom_call_target="tpu_custom_call" | custom-call | tf_op jit(solution)/shard_map/finish/pallas_call | solution.py:517
